TPU v7x, 128 devices: a whole 4x4x4 slice. The times are simulated.
128 devices in a mesh: section: 32 (over x, y_hi, z), tp: 4 (over y_lo, core).
Axes of the slice: x: 4, y: 4 (y_hi: 2, y_lo: 2; y = y_hi * 2 + y_lo), z: 4, core: 2. Of those that a mesh axis runs over, the one named last changes fastest.
Arguments:
- arrivals: bfloat16 [32, 256, 4096], P('section'), may hold values from -6 to 6
- grads_in: bfloat16 [32, 256, 4096], P('section'), may hold values from -6 to 6
- stash: bfloat16 [32, 256, 4096], P('section', 'tp'), may hold values from -6 to 6
- gain: float32 [32, 4096], P('section'), may hold values from 0.1 to 1.9
- w_query: bfloat16 [32, 4096, 4096], P('section', None, 'tp'), as said below
- w_key: bfloat16 [32, 4096, 512], P('section', None, 'tp'), as said below
- w_value: bfloat16 [32, 4096, 512], P('section', None, 'tp'), may hold values from -0.09375 to 0.09375
- w_out: bfloat16 [32, 4096, 4096], P('section', 'tp'), may hold values from -0.09375 to 0.09375
Outputs:
- forward_pass: bfloat16 [32, 256, 4096], P('section')
- backward_pass: bfloat16 [32, 256, 4096], P('section')
- evicted: bfloat16 [32, 256, 4096], P('section', 'tp')
- gain_grad: float32 [32, 4096], P('section')
Inputs may be any that keep to these rules, and one draw needn't show every extreme that they name: `w_query`: each entry has an independent normal part of standard deviation 4096^-0.5; the 8 query heads of a group may in addition share a column block with their group's key head, of a strength of up to 24 times that; every entry's magnitude stays under 200 * 4096^-0.5. `w_key`: each entry has an independent normal part of standard deviation 4096^-0.5, possibly plus a column block shared with the query heads of its group, of the same standard deviation; every entry's magnitude stays under 16 * 4096^-0.5.
All inputs are finite; a program needn't handle non-finite values.
Results may differ from a plain program's by a relative error of at most 0.0087.
Values may be sent and summed in bfloat16 or wider, within the bound.
A program may use at most 128 MiB of HBM per device.

v0:
```python
import math

import jax
import jax.numpy as jnp
from jax import lax
from jax.sharding import PartitionSpec as P

HD = 128


epsilon = 1e-05


def swapped(value, axis, bit):
    mask = 2**bit
    pairs = [(source, source ^ mask) for source in range(lax.axis_size(axis))]
    return lax.ppermute(value, axis, pairs)


def from_behind(value, axis, steps):
    count = lax.axis_size(axis)
    leading, last = (max(0, -steps), min(count, count - steps))
    return lax.ppermute(value, axis, [(source, source + steps) for source in range(leading, last)])


def rotate(heads, sign):
    length = heads.shape[0]
    half = heads.shape[2] // 2
    positions = jnp.arange(length).astype(jnp.float32)
    frequency = jnp.exp(
        jnp.arange(half).astype(jnp.float32) * (-2.0 * math.log(10000.0) / heads.shape[2])
    )
    angle = positions[:, None] * frequency[None, :]
    cosine = jnp.cos(angle)[:, None, :]
    sine = sign * jnp.sin(angle)[:, None, :]
    first = heads[..., :half]
    second = heads[..., half:]
    return jnp.concatenate(
        [first * cosine - second * sine, second * cosine + first * sine], axis=-1
    )


def normalize(inputs, gain):
    values = inputs.astype(jnp.float32)
    inverse_rms = lax.rsqrt(jnp.mean(values * values, axis=-1, keepdims=True) + epsilon)
    scaled = values * inverse_rms
    return (scaled, inverse_rms, (scaled * gain).astype(jnp.bfloat16))


def project(normed, w_query, w_key, w_value):
    length = normed.shape[0]
    query_heads = jnp.dot(normed, w_query, preferred_element_type=jnp.float32).reshape(
        length, -1, HD
    )
    key_heads = jnp.dot(normed, w_key, preferred_element_type=jnp.float32).reshape(length, -1, HD)
    value_heads = jnp.dot(normed, w_value, preferred_element_type=jnp.float32).reshape(
        length, -1, HD
    )
    return (
        rotate(query_heads, 1.0).astype(jnp.bfloat16),
        rotate(key_heads, 1.0).astype(jnp.bfloat16),
        value_heads.astype(jnp.bfloat16),
    )


def attend(query_heads, key_heads):
    length = query_heads.shape[0]
    groups = key_heads.shape[1]
    grouped = query_heads.reshape(length, groups, -1, HD)
    scores = jnp.einsum(
        "qkge,ske->kgqs", grouped, key_heads, preferred_element_type=jnp.float32
    ) * HD ** (-0.5)
    causal = jnp.arange(length)[:, None] >= jnp.arange(length)[None, :]
    scores = jnp.where(causal, scores, -jnp.inf)
    highest = jnp.max(scores, axis=-1, keepdims=True)
    weights = jnp.exp(scores - highest)
    return weights / jnp.sum(weights, axis=-1, keepdims=True)


def transposed(left, weight):
    return lax.dot_general(
        left, weight, (((1,), (1,)), ((), ())), preferred_element_type=jnp.float32
    )


def input_term(d_query, d_key, d_value, w_query, w_key, w_value):
    summed = transposed(d_query, w_query) + transposed(d_key, w_key)
    return summed + transposed(d_value, w_value)


def norm_back(d_normed, scaled, inverse_rms, gradient, gain):
    d_gain = jnp.sum(d_normed * scaled, axis=0)
    d_unit = d_normed * gain
    d_inputs = gradient.astype(jnp.float32) + inverse_rms * (
        d_unit - scaled * jnp.mean(d_unit * scaled, axis=-1, keepdims=True)
    )
    return (d_inputs.astype(jnp.bfloat16), d_gain)


def shards(arrivals, grads_in, stash, gain, w_query, w_key, w_value, w_out):
    incoming = arrivals[0]
    upstream = grads_in[0]
    held = stash[0]
    section_gain = gain[0]
    query_w = w_query[0]
    key_w = w_key[0]
    value_w = w_value[0]
    out_w = w_out[0]
    length = incoming.shape[0]
    share_rows = held.shape[0]
    first_row = lax.axis_index("tp") * share_rows
    leaving = lax.dynamic_slice_in_dim(incoming, first_row, share_rows, 0)
    hop_count = lax.axis_size("section").bit_length() - 1
    assembled = lax.all_gather(held, "tp", axis=0, tiled=True)
    carried = jnp.concatenate([assembled, leaving], axis=0)
    for bit_index in range(hop_count):
        carried = swapped(carried, "section", bit_index)
    stored = carried[:length]
    evicted = carried[length:]
    scaled_f, inverse_f, normed_f = normalize(incoming, section_gain)
    query_f, key_f, value_f = project(normed_f, query_w, key_w, value_w)
    attention_f = attend(query_f, key_f).astype(jnp.bfloat16)
    context = jnp.einsum("kgqs,ske->qkge", attention_f, value_f, preferred_element_type=jnp.float32)
    context = context.reshape(length, -1).astype(jnp.bfloat16)
    scaled_b, inverse_b, normed_b = normalize(stored, section_gain)
    query_b, key_b, value_b = project(normed_b, query_w, key_w, value_w)
    attention_b = attend(query_b, key_b)
    attention_low = attention_b.astype(jnp.bfloat16)
    groups = key_b.shape[1]
    grouped = query_b.reshape(length, groups, -1, HD)
    d_context = transposed(upstream, out_w).astype(jnp.bfloat16).reshape(length, groups, -1, HD)
    d_probs = jnp.einsum("qkge,ske->kgqs", d_context, value_b, preferred_element_type=jnp.float32)
    d_scores = (
        attention_b
        * (d_probs - jnp.sum(attention_b * d_probs, axis=-1, keepdims=True))
        * HD ** (-0.5)
    )
    d_scores = d_scores.astype(jnp.bfloat16)
    d_query = jnp.einsum(
        "kgqs,ske->qkge", d_scores, key_b, preferred_element_type=jnp.float32
    ).reshape(length, -1, HD)
    d_key = jnp.einsum("kgqs,qkge->ske", d_scores, grouped, preferred_element_type=jnp.float32)
    d_value = jnp.einsum(
        "kgqs,qkge->ske", attention_low, d_context, preferred_element_type=jnp.float32
    )
    d_query = rotate(d_query, -1.0).astype(jnp.bfloat16).reshape(length, -1)
    d_key = rotate(d_key, -1.0).astype(jnp.bfloat16).reshape(length, -1)
    d_value = d_value.astype(jnp.bfloat16).reshape(length, -1)
    summed = lax.psum(jnp.dot(context, out_w, preferred_element_type=jnp.float32), "tp")
    result = (incoming.astype(jnp.float32) + summed).astype(jnp.bfloat16)
    forward_out = from_behind(result, "section", 1)
    d_normed = lax.psum(input_term(d_query, d_key, d_value, query_w, key_w, value_w), "tp")
    d_inputs, d_gain = norm_back(d_normed, scaled_b, inverse_b, upstream, section_gain)
    behind = from_behind(d_inputs, "section", -1)
    return (forward_out[None], behind[None], evicted[None], d_gain[None])


def solution(mesh):
    in_specs = (
        P("section", None, None),
        P("section", None, None),
        P("section", "tp", None),
        P("section", None),
        P("section", None, "tp"),
        P("section", None, "tp"),
        P("section", None, "tp"),
        P("section", "tp", None),
    )
    out_specs = (
        P("section", None, None),
        P("section", None, None),
        P("section", "tp", None),
        P("section", None),
    )
    return jax.shard_map(shards, mesh=mesh, in_specs=in_specs, out_specs=out_specs, check_vma=False)
```

profile of v0, /device:TPU:1, one launch (start us, length us, event | category | flops | bytes accessed | tf_op | source)
XLA Modules:
  0.0 621.0 jit_solution(10905636174197211140)
XLA Ops:
  7.2 0.0 copy-start
  7.2 0.0 all-gather.3.cloned.1.call-start
  7.2 0.7 all-gather.3.cloned.1.call-update
  7.9 0.0 all-reduce.3.cloned.1.call-start
  8.0 1.1 dynamic-slice_bitcast_fusion
  9.0 33.4 %all-gather.3.cloned.1.call-done = bf16[1,256,4096]{2,1,0:T(8,128)(2,1)} async-done(((bf16[1,64,4096]{2,1,0:T(8,128)(2,1)}), bf16[1,256,4096]{2,1,0:T(8,128)(2,1)}) %all-gather.3.cloned.1.call-update) | async-done | bytes 2097168 | tf_op jit(solution)/shard_map/all_gather | solution.py:114
  42.4 1.8 pad_maximum_fusion
  44.2 1.4 collective-permute-start.1
  45.6 57.2 %collective-permute-done.1 = bf16[320,4096]{1,0:T(8,128)(2,1)S(1)} collective-permute-done((bf16[320,4096]{1,0:T(8,128)(2,1)S(1)}, bf16[320,4096]{1,0:T(8,128)(2,1)S(1)}, u32[]{:S(2)}, u32[]{:S(2)}) %collective-permute-start.1) | collective-permute-done | bytes 2621472 | tf_op jit(solution)/shard_map/ppermute | solution.py:17
  102.8 2.9 collective-permute-start.2
  105.6 56.2 %collective-permute-done.2 = bf16[320,4096]{1,0:T(8,128)(2,1)S(1)} collective-permute-done((bf16[320,4096]{1,0:T(8,128)(2,1)S(1)}, bf16[320,4096]{1,0:T(8,128)(2,1)S(1)}, u32[]{:S(2)}, u32[]{:S(2)}) %collective-permute-start.2) | collective-permute-done | bytes 2621472 | tf_op jit(solution)/shard_map/ppermute | solution.py:17
  161.8 2.4 collective-permute-start.3
  164.2 55.8 %collective-permute-done.3 = bf16[320,4096]{1,0:T(8,128)(2,1)} collective-permute-done((bf16[320,4096]{1,0:T(8,128)(2,1)S(1)}, bf16[320,4096]{1,0:T(8,128)(2,1)}, u32[]{:S(2)}, u32[]{:S(2)}) %collective-permute-start.3) | collective-permute-done | bytes 2621472 | tf_op jit(solution)/shard_map/ppermute | solution.py:17
  220.0 1.2 collective-permute-start.4
  221.2 11.5 %copy.36 = bf16[1024,4096]{1,0:T(8,128)(2,1)} copy(bf16[1024,4096]{0,1:T(8,128)(2,1)} %bitcast.197) | data formatting | bytes 16777216 | tf_op jit(solution)/shard_map/dot_general | solution.py:52
  232.7 43.4 %collective-permute-done.4 = bf16[320,4096]{1,0:T(8,128)(2,1)} collective-permute-done((bf16[320,4096]{1,0:T(8,128)(2,1)}, bf16[320,4096]{1,0:T(8,128)(2,1)}, u32[]{:S(2)}, u32[]{:S(2)}) %collective-permute-start.4) | collective-permute-done | bytes 2621472 | tf_op jit(solution)/shard_map/ppermute | solution.py:17
  276.0 2.7 collective-permute-start.5
  278.7 6.5 %fusion.40 = bf16[256,1024]{1,0:T(8,128)(2,1)S(1)} fusion(bf16[1,1024,4096]{2,1,0:T(8,128)(2,1)} %param.15, bf16[1,256,4096]{2,1,0:T(8,128)(2,1)} %param.9), kind=kOutput, calls=%fused_computation.55 | convolution fusion | flops 2147745792 | bytes 11010048 | tf_op jit(solution)/shard_map/dot_general | solution.py:81
  285.3 0.0 copy-start.12
  285.3 0.0 copy-start.10
  285.3 0.0 copy-start.21
  285.3 0.9 copy.38
  286.3 0.5 fusion.20
  286.8 0.3 broadcast_multiply_fusion
  287.1 1.6 fusion.45
  288.7 2.4 fusion.31
  291.2 42.9 %collective-permute-done.5 = bf16[320,4096]{1,0:T(8,128)(2,1)S(1)} collective-permute-done((bf16[320,4096]{1,0:T(8,128)(2,1)}, bf16[320,4096]{1,0:T(8,128)(2,1)S(1)}, u32[]{:S(2)}, u32[]{:S(2)}) %collective-permute-start.5) | collective-permute-done | bytes 2621472 | tf_op jit(solution)/shard_map/ppermute | solution.py:17
  334.1 0.5 fusion.19
  334.6 1.0 convolution_bitcast_fusion.1
  335.6 0.3 fusion.108
  336.0 2.4 fusion.28
  338.4 1.0 subtract_convert_fusion.1
  339.4 0.7 copy-done.13
  340.1 0.5 fusion.126
  340.6 0.0 copy-start.5
  340.6 1.3 copy-done.5
  341.9 0.9 fusion.39
  342.8 5.7 fusion.24
  348.6 4.0 convert_bitcast_fusion.1
  352.5 0.3 convolution_bitcast_fusion
  352.8 1.1 convolution_bitcast_fusion.3
  354.0 0.1 subtract_convert_fusion
  354.2 7.7 %fusion.4 = f32[256,4096]{1,0:T(8,128)} fusion(bf16[256,1024]{0,1:T(8,128)(2,1)S(1)} %bitcast.206, bf16[1,4096,1024]{2,1,0:T(8,128)(2,1)} %param.12), kind=kOutput, calls=%fused_computation.4 | convolution fusion | flops 2147483648 | bytes 13107200 | tf_op jit(solution)/shard_map/dot_general | solution.py:81
  361.9 2.6 copy.32
  364.6 1.3 fusion.112
  365.9 1.4 fusion.131
  367.3 1.3 copy-done.8
  368.6 0.3 fusion.37
  368.9 3.7 convolution_convert_fusion
  372.7 8.1 %fusion.2 = f32[256,4096]{1,0:T(8,128)} fusion(bf16[256,1024]{0,1:T(8,128)(2,1)} %bitcast.204, bf16[1,1024,4096]{2,1,0:T(8,128)(2,1)} %param.15), kind=kOutput, calls=%fused_computation.2 | convolution fusion | flops 2147483648 | bytes 13107200 | tf_op jit(solution)/shard_map/dot_general | solution.py:149
  380.8 2.7 convolution_add_fusion.1
  383.4 5.9 convolution_add_fusion
  389.3 0.0 all-reduce.3.cloned.1.call-update
  389.4 163.0 %all-reduce.3.cloned.1.call-done = (f32[256,4096]{1,0:T(8,128)}, f32[256,4096]{1,0:T(8,128)}) async-done(((f32[256,4096]{1,0:T(8,128)}, f32[256,4096]{1,0:T(8,128)}), (f32[256,4096]{1,0:T(8,128)}, f32[256,4096]{1,0:T(8,128)})) %all-reduce.3.cloned.1.call-update) | async-done | bytes 8388624 | tf_op jit(solution)/shard_map/psum | solution.py:149
  552.4 4.9 fusion.18
  557.2 3.9 fusion.17
  561.2 1.3 collective-permute-start.6
  562.5 0.6 fusion.21
  563.1 4.1 collective-permute-start
  567.2 0.8 slice_bitcast_fusion
  568.1 42.0 %collective-permute-done.6 = bf16[256,4096]{1,0:T(8,128)(2,1)S(1)} collective-permute-done((bf16[256,4096]{1,0:T(8,128)(2,1)S(1)}, bf16[256,4096]{1,0:T(8,128)(2,1)S(1)}, u32[]{:S(2)}, u32[]{:S(2)}) %collective-permute-start.6) | collective-permute-done | bytes 2097184 | tf_op jit(solution)/shard_map/ppermute | solution.py:23
  610.0 1.5 collective-permute-done
  611.5 1.3 copy.49
  612.8 1.3 copy.50
  (61 shorter events, 0.2 us)
Async XLA Ops:
  7.2 335.7 %copy-start = (bf16[1,4096,128]{2,1,0:T(8,128)(2,1)S(1)}, bf16[1,4096,128]{2,1,0:T(8,128)(2,1)}, u32[]{:S(2)}) copy-start(bf16[1,4096,128]{2,1,0:T(8,128)(2,1)} %param.14) | copy-start | bytes 3145732
  7.2 35.3 %all-gather.3.cloned.1.call-start = ((), (), s32[]{:S(2)}) async-start(), calls=%async_computation | async-start | bytes 2621440 | tf_op jit(solution)/shard_map/all_gather | solution.py:114
  7.9 544.4 %all-reduce.3.cloned.1.call-start = ((), (), s32[]{:S(2)}) async-start(), calls=%async_computation.1 | async-start | bytes 16777216 | tf_op jit(solution)/shard_map/psum | solution.py:149
  44.2 58.5 %collective-permute-start.1 = (bf16[320,4096]{1,0:T(8,128)(2,1)S(1)}, bf16[320,4096]{1,0:T(8,128)(2,1)S(1)}, u32[]{:S(2)}, u32[]{:S(2)}) collective-permute-start(bf16[320,4096]{1,0:T(8,128)(2,1)S(1)} %pad_maximum_fusion), channel_id=1, source_target_pairs={{0,4},{4,0},{8,12},{12,8},{16,20},{20,16},{24,28},{28,24},{32,36},... | collective-permute-start | bytes 7864328 | tf_op jit(solution)/shard_map/ppermute | solution.py:17
  102.8 59.0 %collective-permute-start.2 = (bf16[320,4096]{1,0:T(8,128)(2,1)S(1)}, bf16[320,4096]{1,0:T(8,128)(2,1)S(1)}, u32[]{:S(2)}, u32[]{:S(2)}) collective-permute-start(bf16[320,4096]{1,0:T(8,128)(2,1)S(1)} %collective-permute-done.1), channel_id=1, source_target_pairs={{0,8},{4,12},{8,0},{12,4},{16,24},{20,28},{24,16},{28,20},{32,40},... | collective-permute-start | bytes 7864328 | tf_op jit(solution)/shard_map/ppermute | solution.py:17
  161.8 58.2 %collective-permute-start.3 = (bf16[320,4096]{1,0:T(8,128)(2,1)S(1)}, bf16[320,4096]{1,0:T(8,128)(2,1)}, u32[]{:S(2)}, u32[]{:S(2)}) collective-permute-start(bf16[320,4096]{1,0:T(8,128)(2,1)S(1)} %collective-permute-done.2), channel_id=1, source_target_pairs={{0,16},{4,20},{8,24},{12,28},{16,0},{20,4},{24,8},{28,12},{32,48},... | collective-permute-start | bytes 7864328 | tf_op jit(solution)/shard_map/ppermute | solution.py:17
  220.0 56.0 %collective-permute-start.4 = (bf16[320,4096]{1,0:T(8,128)(2,1)}, bf16[320,4096]{1,0:T(8,128)(2,1)}, u32[]{:S(2)}, u32[]{:S(2)}) collective-permute-start(bf16[320,4096]{1,0:T(8,128)(2,1)} %collective-permute-done.3), channel_id=1, source_target_pairs={{0,32},{4,36},{8,40},{12,44},{16,48},{20,52},{24,56},{28,60},{32,0... | collective-permute-start | bytes 7864328 | tf_op jit(solution)/shard_map/ppermute | solution.py:17
  232.7 53.6 %copy-start.3 = (bf16[1,256,4096]{2,1,0:T(8,128)(2,1)S(1)}, bf16[1,256,4096]{2,1,0:T(8,128)(2,1)}, u32[]{:S(2)}) copy-start(bf16[1,256,4096]{2,1,0:T(8,128)(2,1)} %param.8) | copy-start | bytes 6291460
  276.0 58.1 %collective-permute-start.5 = (bf16[320,4096]{1,0:T(8,128)(2,1)}, bf16[320,4096]{1,0:T(8,128)(2,1)S(1)}, u32[]{:S(2)}, u32[]{:S(2)}) collective-permute-start(bf16[320,4096]{1,0:T(8,128)(2,1)} %collective-permute-done.4), channel_id=1, source_target_pairs={{0,64},{4,68},{8,72},{12,76},{16,80},{20,84},{24,88},{28,92},{32,9... | collective-permute-start | bytes 7864328 | tf_op jit(solution)/shard_map/ppermute | solution.py:17
  278.7 10.0 %copy-start.4 = (bf16[1024,4096]{1,0:T(8,128)(2,1)S(1)}, bf16[1024,4096]{1,0:T(8,128)(2,1)}, u32[]{:S(2)}) copy-start(bf16[1024,4096]{1,0:T(8,128)(2,1)} %copy.36) | copy-start | bytes 25165828
  285.3 3.5 copy-start.12
  285.3 1.8 copy-start.10
  285.3 1.8 copy-start.21
  286.2 49.4 %copy-start.29 = (f32[64]{0:T(128)}, f32[64]{0:T(128)S(1)}, u32[]{:S(2)}) copy-start(f32[64]{0:T(128)S(1)} %multiply_exponential_fusion) | copy-start | bytes 772
  286.2 49.4 %copy-start.25 = (f32[256]{0:T(256)}, f32[256]{0:T(256)S(1)}, u32[]{:S(2)}) copy-start(f32[256]{0:T(256)S(1)} %iota_convert_fusion) | copy-start | bytes 3076
  286.3 53.1 %copy-start.22 = (pred[256,256]{0,1:T(8,128)(4,1)}, pred[256,256]{0,1:T(8,128)(4,1)S(1)}, u32[]{:S(2)}) copy-start(pred[256,256]{0,1:T(8,128)(4,1)S(1)} %iota_compare_fusion) | copy-start | bytes 196612
  286.8 4.4 copy-start.30
  334.1 1.8 copy-start.1
  334.6 1.3 copy-start.26
  335.9 3.5 copy-start.17
  336.0 3.5 copy-start.19
  339.4 0.7 copy-start.13
  339.4 1.2 copy-start.15
  340.6 1.3 copy-start.5
  340.6 1.3 copy-start.24
  348.5 4.0 copy-start.18
  348.5 4.0 copy-start.20
  348.5 4.3 copy-start.14
  348.6 4.3 copy-start.16
  354.2 11.7 %copy-start.23 = (pred[256,256]{0,1:T(8,128)(4,1)S(1)}, pred[256,256]{0,1:T(8,128)(4,1)}, u32[]{:S(2)}) copy-start(pred[256,256]{0,1:T(8,128)(4,1)} %copy-done.22) | copy-start | bytes 196612
  367.3 1.3 copy-start.8
  367.3 1.3 copy-start.28
  372.7 8.1 %copy-start.6 = (f32[256,4096]{1,0:T(8,128)S(1)}, f32[256,4096]{1,0:T(8,128)}, u32[]{:S(2)}) copy-start(f32[256,4096]{1,0:T(8,128)} %fusion.4) | copy-start | bytes 12582916
  372.7 8.1 %copy-start.11 = (bf16[1,4096,128]{2,1,0:T(8,128)(2,1)S(1)}, bf16[1,4096,128]{2,1,0:T(8,128)(2,1)}, u32[]{:S(2)}) copy-start(bf16[1,4096,128]{2,1,0:T(8,128)(2,1)} %param.13) | copy-start | bytes 3145732
  389.3 163.0 %copy-start.27 = (f32[256]{0:T(256)S(1)}, f32[256]{0:T(256)}, u32[]{:S(2)}) copy-start(f32[256]{0:T(256)} %copy-done.26) | copy-start | bytes 3076
  552.4 4.9 copy-start.2
  552.4 4.9 copy-start.9
  557.2 5.2 copy-start.7
  561.2 48.8 %collective-permute-start.6 = (bf16[256,4096]{1,0:T(8,128)(2,1)S(1)}, bf16[256,4096]{1,0:T(8,128)(2,1)S(1)}, u32[]{:S(2)}, u32[]{:S(2)}) collective-permute-start(bf16[256,4096]{1,0:T(8,128)(2,1)S(1)} %fusion.17), channel_id=1, source_target_pairs={{4,0},{8,4},{12,8},{16,12},{20,16},{24,20},{28,24},{32,28},{36,32}... | collective-permute-start | bytes 6291464 | tf_op jit(solution)/shard_map/ppermute | solution.py:23
  563.1 48.4 %collective-permute-start = (bf16[256,4096]{1,0:T(8,128)(2,1)S(1)}, bf16[256,4096]{1,0:T(8,128)(2,1)S(1)}, u32[]{:S(2)}, u32[]{:S(2)}) collective-permute-start(bf16[256,4096]{1,0:T(8,128)(2,1)S(1)} %fusion.21), channel_id=1, source_target_pairs={{0,4},{4,8},{8,12},{12,16},{16,20},{20,24},{24,28},{28,32},{32,36}... | collective-permute-start | bytes 6291464 | tf_op jit(solution)/shard_map/ppermute | solution.py:23
Sparse Core Ops, SparseCore 0:
  9.7 32.7 all-gather.2
  389.5 162.8 all-reduce.2
where the time goes:
time: 632 us; the launch traced here: 621 us
  waiting for transfers between devices  496 us (78%)
  matrix products  51.2 us (8%)
  local copies, waits for them, and re-layouts  22.9 us (4%)
  other arithmetic  20.4 us (3%)
  starting transfers between devices  16.1 us (3%)
  between operations  14.4 us (2%)
    ppermute x5, waiting for transfers between devices, swapped(): return lax.ppermute(value, axis, pairs)  255 us
    psum x1, waiting for transfers between devices, shards(): lax.psum(jnp.dot(context, out_w, preferred_element_type=jnp.float32), 'tp')  163 us
    ppermute x2, waiting for transfers between devices, from_behind(): lax.ppermute(value, axis, [(source, source + steps) for source in range(l...  43.5 us
    all_gather x1, waiting for transfers between devices, shards(): assembled = lax.all_gather(held, 'tp', axis=0, tiled=True)  33.4 us
    dot_general x4, matrix products, transposed(): lax.dot_general(left, weight, (((1,), (1,)), ((), ())), preferred_element...  22.8 us
  transfers between devices with their start and end apart: 9, of which 9 were waited for; matrix products, arithmetic and copies ran while one was open for 4% of the time, Pallas kernels for 0%

commit v1 on v0

v1 whole, which is shorter than its diff:
```python
import functools

import jax
import jax.numpy as jnp
import numpy as np
from jax import lax
from jax.experimental import pallas as pl
from jax.experimental.pallas import tpu as pltpu
from jax.sharding import PartitionSpec as P

HD = 128
NC = 8
EPSILON = 1e-05
MESH = pl.DeviceIdType.MESH
NN = (((1,), (0,)), ((), ()))
NT = (((1,), (1,)), ((), ()))
TN = (((0,), (0,)), ((), ()))

ST_M, ST_C, ST_L, ST_F = 0, 1, 2, 3
RS_C, RS_L, HOP, AG_C, AG_L, AG_F = 4, 5, 6, 7, 8, 9
PASS = 6
KINDS = 16


def dot(left, right, dims=NN):
    return lax.dot_general(left, right, dims, preferred_element_type=jnp.float32)


def rope_tables(length):
    half = HD // 2
    frequency = np.exp(np.arange(half, dtype=np.float32) * np.float32(-2.0 * np.log(10000.0) / HD))
    angle = np.arange(length, dtype=np.float32)[:, None] * frequency.astype(np.float32)[None, :]
    cosine, sine = np.cos(angle), np.sin(angle)
    return np.stack(
        [np.concatenate([cosine, cosine], 1), np.concatenate([-sine, sine], 1)]
    ).astype(np.float32)


def kernel(
    sections, tokens, width, heads,
    arr, grd, sth, gain, wq, wk, wv, wo, rope,
    out_f, out_b, evict, out_g,
    w, wob, zf, g, zb, nrm, qkv, ctx, dctx, dqkv, mine, dk, dv, gn, rp, scl, inv, dn, dot_sum,
    sc, rc, sl, rl, hop, gp, gr,
    loc_sem, send_sem, recv_sem, ev_sem, gp_sem,
):
    nq = heads * HD
    rows = tokens // 4
    cw = width // NC
    s = lax.axis_index("section")
    t = lax.axis_index("tp")
    t_core = t + 1 - 2 * (t % 2)
    t_lo = (t + 2) % 4
    t_diag = (t_core + 2) % 4
    last_z = (s % 4) // 3
    first_z = ((s + 3) % 4) // 3
    t_next = (t + 2 * last_z) % 4
    t_prev = (t + 2 * first_z) % 4
    p_core = (s, t_core)
    p_lo = (s, t_lo)
    p_mir = (sections - 1 - s, t_lo)
    p_next = ((s + 1) % sections, t_next)
    p_prev = ((s + sections - 1) % sections, t_prev)

    def block(index):
        return pl.ds(pl.multiple_of(index * rows, rows), rows)

    def chunk(n):
        return pl.ds(pl.multiple_of(n * cw, cw), cw)

    def remote(src, dst, kind, n, device):
        return pltpu.make_async_remote_copy(
            src_ref=src, dst_ref=dst, send_sem=send_sem.at[kind, n], recv_sem=recv_sem.at[kind, n],
            device_id=device, device_id_type=MESH,
        )

    tile = 256
    tiles = nq // tile

    def load(src, dst, n):
        return pltpu.make_async_copy(src, dst, loc_sem.at[n])

    loads = [
        load(arr.at[0], zf, 0),
        load(gain, gn, 1),
        load(wk.at[0], w.at[:, pl.ds(nq, HD)], 2),
        load(wv.at[0], w.at[:, pl.ds(nq + HD, HD)], 3),
        load(rope, rp, 4),
        load(grd.at[0], g, 5),
        load(wo.at[0], wob, 6),
    ]

    def load_q(n):
        cols = pl.ds(pl.multiple_of(n * tile, tile), tile)
        return load(wq.at[0, :, cols], w.at[:, cols], 7 + n)

    loads[0].start()
    loads[1].start()
    loads[4].start()
    for n in range(tiles):
        load_q(n).start()
    loads[2].start()
    loads[3].start()
    loads[5].start()
    loads[6].start()

    barrier = pltpu.get_barrier_semaphore()
    for device in (p_core, p_lo, p_mir, p_next, p_prev):
        pl.semaphore_signal(barrier, inc=1, device_id=device, device_id_type=MESH)
    pl.semaphore_wait(barrier, 5)

    def st_m(n, at):
        return remote(sth.at[0, :, chunk(n)], zb.at[block(at), chunk(n)], ST_M, n, p_mir)

    def st_c(n, at):
        return remote(zb.at[block(t_lo), chunk(n)], zb.at[block(at), chunk(n)], ST_C, n, p_core)

    def st_l(n, at):
        return remote(zb.at[block(t_lo), chunk(n)], zb.at[block(at), chunk(n)], ST_L, n, p_lo)

    def st_f(n, at):
        return remote(zb.at[block(t), chunk(n)], zb.at[block(at), chunk(n)], ST_F, n, p_core)

    def each(count, body):
        lax.fori_loop(0, count, lambda i, c: (body(i), c)[1], 0)

    each(NC, lambda n: st_m(n, t).start())

    def stash_spread(n):
        st_m(n, t_lo).wait_recv()
        st_l(n, t_lo).start()
        st_c(n, t_lo).start()

    def stash_forward(n):
        st_l(n, t).wait_recv()
        st_f(n, t).start()

    def stash_last(n):
        st_c(n, t_diag).wait_recv()
        st_f(n, t_core).wait_recv()

    evicted = pltpu.make_async_remote_copy(
        src_ref=arr.at[0, block(t_lo)], dst_ref=evict.at[0], send_sem=ev_sem.at[0],
        recv_sem=ev_sem.at[1], device_id=p_mir, device_id_type=MESH,
    )

    step = 16

    def normalize(src):
        def body(i):
            at = pl.ds(pl.multiple_of(i * step, step), step)
            x = src[at].astype(jnp.float32)
            inverse = lax.rsqrt(jnp.mean(x * x, axis=-1, keepdims=True) + EPSILON)
            x = src[at].astype(jnp.float32)
            nrm[at] = (x * inverse * gn[...]).astype(jnp.bfloat16)

        each(tokens // step, body)

    def turn(x, sign):
        return x * rp[0] + pltpu.roll(x, HD // 2, 1) * (sign * rp[1])

    def project_q(n):
        cols = pl.ds(pl.multiple_of(n * tile, tile), tile)
        y = dot(nrm[...], w[:, cols])
        y = jnp.concatenate(
            [turn(y[:, i * HD:(i + 1) * HD], 1.0) for i in range(tile // HD)], axis=1
        )
        qkv[:, cols] = y.astype(jnp.bfloat16)

    def project_kv():
        y = dot(nrm[...], w[:, nq:])
        qkv[:, nq:nq + HD] = turn(y[:, :HD], 1.0).astype(jnp.bfloat16)
        qkv[:, nq + HD:] = y[:, HD:].astype(jnp.bfloat16)

    def place(b):
        low = (b % 2 + t % 2) % 2
        high = (b // 2 + t // 2) % 2
        return block(2 * low + high)

    def put(ref, cols, value):
        for b in range(4):
            ref[place(b), cols] = value[b * rows:(b + 1) * rows]

    def head_cols(h):
        return pl.ds(pl.multiple_of(h * HD, HD), HD)

    scale = HD ** (-0.5)

    def attend(h):
        cols = head_cols(h)
        scores = dot(qkv[:, cols], qkv[:, nq:nq + HD], NT) * scale
        q_at = lax.broadcasted_iota(jnp.int32, scores.shape, 0)
        k_at = lax.broadcasted_iota(jnp.int32, scores.shape, 1)
        scores = jnp.where(q_at >= k_at, scores, -jnp.inf)
        e = jnp.exp(scores - jnp.max(scores, axis=1, keepdims=True))
        probs = e / jnp.sum(e, axis=1, keepdims=True)
        out = dot(probs.astype(jnp.bfloat16), qkv[:, nq + HD:])
        put(ctx, cols, out.astype(jnp.bfloat16))

    def attend_back(h):
        cols = head_cols(h)
        q, k, v = qkv[:, cols], qkv[:, nq:nq + HD], qkv[:, nq + HD:]
        dc = dctx[:, cols]
        scores = dot(k, q, NT) * scale
        k_at = lax.broadcasted_iota(jnp.int32, scores.shape, 0)
        q_at = lax.broadcasted_iota(jnp.int32, scores.shape, 1)
        scores = jnp.where(q_at >= k_at, scores, -jnp.inf)
        e = jnp.exp(scores - jnp.max(scores, axis=0, keepdims=True))
        probs = e / jnp.sum(e, axis=0, keepdims=True)
        d_probs = dot(v, dc, NT)
        inner = jnp.sum(probs * d_probs, axis=0, keepdims=True)
        d_scores = (probs * (d_probs - inner) * scale).astype(jnp.bfloat16)
        dk[...] += dot(d_scores, q)
        dv[...] += dot(probs.astype(jnp.bfloat16), dc)
        put(dqkv, cols, turn(dot(d_scores, k, TN), -1.0).astype(jnp.bfloat16))

    def context_back(n):
        cols = pl.ds(pl.multiple_of(n * tile, tile), tile)
        dctx[:, cols] = dot(g[...], wob[cols, :], NT).astype(jnp.bfloat16)

    def rs_core(f, n):
        return remote(sc.at[f, n], rc.at[f, n], RS_C + PASS * f, n, p_core)

    def rs_lo(f, n):
        return remote(sl.at[f, n], rl.at[f, n], RS_L + PASS * f, n, p_lo)

    def sum_send(f, n, part):
        sc[f, n] = part[2 * rows:].astype(jnp.bfloat16)
        rs_core(f, n).start()
        mine[:, chunk(n)] = part[:2 * rows]

    def sum_core(f, n):
        rs_core(f, n).wait_recv()
        total = mine[:, chunk(n)] + rc[f, n].astype(jnp.float32)
        sl[f, n] = total[rows:].astype(jnp.bfloat16)
        rs_lo(f, n).start()
        mine[:rows, chunk(n)] = total[:rows]

    def sum_lo(f, n):
        rs_lo(f, n).wait_recv()
        return mine[:rows, chunk(n)] + rl[f, n].astype(jnp.float32)

    outs = (out_f, out_b)
    hops = (p_next, p_prev)
    came = ((t + 2 * first_z) % 4, (t + 2 * last_z) % 4)

    def at_out(f, b, n):
        return outs[f].at[0, block(b), chunk(n)]

    def hop_copy(f, n, b):
        return remote(hop.at[f, :, chunk(n)], at_out(f, b, n), HOP + PASS * f, n, hops[f])

    def ag(f, n, kind, b, to):
        return remote(at_out(f, b, n), at_out(f, b, n), kind + PASS * f, n, to)

    def flip_core(b):
        return b + 1 - 2 * (b % 2)

    def flip_lo(b):
        return (b + 2) % 4

    def spread(f, n):
        b = came[f]
        hop_copy(f, n, b).wait_recv()
        ag(f, n, AG_L, b, p_lo).start()
        ag(f, n, AG_C, b, p_core).start()

    def forward(f, n):
        b = flip_lo(came[f])
        ag(f, n, AG_L, b, p_lo).wait_recv()
        ag(f, n, AG_F, b, p_core).start()

    def collect(f, n):
        b = flip_core(came[f])
        ag(f, n, AG_C, b, p_core).wait_recv()
        ag(f, n, AG_F, flip_lo(b), p_core).wait_recv()

    def finish_f(n):
        y = zf[block(t), chunk(n)].astype(jnp.float32) + sum_lo(0, n)
        y = jnp.where(s == sections - 1, jnp.zeros_like(y), y)
        hop[0, :, chunk(n)] = y.astype(jnp.bfloat16)
        hop_copy(0, n, t).start()

    loads[0].wait()
    loads[1].wait()
    normalize(zf)
    loads[4].wait()

    def run_project(i):
        load_q(i).wait()
        project_q(i)
        stash_spread(i)

    each(tiles, run_project)
    loads[2].wait()
    loads[3].wait()
    project_kv()
    loads[5].wait()
    loads[6].wait()

    def run_context_back(i):
        context_back(i)
        stash_spread(NC - tiles + i)

    each(tiles, run_context_back)
    evicted.start()

    def run_attend(h):
        attend(h)
        stash_forward(h)

    each(heads, run_attend)

    def run_out(n):
        sum_send(0, n, dot(ctx[...], wob[:, chunk(n)]))

        @pl.when(n > 0)
        def _():
            sum_core(0, n - 1)

    each(NC, run_out)
    sum_core(0, NC - 1)

    each(NC, stash_last)
    normalize(zb)

    def run_project_b(i):
        project_q(i)
        finish_f(i)

    each(tiles, run_project_b)
    project_kv()
    dk[...] = jnp.zeros_like(dk)
    dv[...] = jnp.zeros_like(dv)

    def run_attend_back(h):
        attend_back(h)

        @pl.when(h < NC - tiles)
        def _():
            finish_f(tiles + h)

        spread(0, h)

    each(heads, run_attend_back)
    put(dqkv, pl.ds(nq, HD), turn(dk[...], -1.0).astype(jnp.bfloat16))
    put(dqkv, pl.ds(nq + HD, HD), dv[...].astype(jnp.bfloat16))

    def run_d_normed(n):
        sum_send(1, n, dot(dqkv[...], w[chunk(n), :], NT))

        @pl.when(n > 0)
        def _():
            sum_core(1, n - 1)

        forward(0, n)

    each(NC, run_d_normed)
    sum_core(1, NC - 1)

    def own_scaled(i):
        at = pl.ds(pl.multiple_of(t * rows + i * step, step), step)
        to = pl.ds(pl.multiple_of(i * step, step), step)
        x = zb[at].astype(jnp.float32)
        inverse = lax.rsqrt(jnp.mean(x * x, axis=-1, keepdims=True) + EPSILON)
        x = zb[at].astype(jnp.float32)
        scl[to] = x * inverse
        inv[to] = jnp.broadcast_to(inverse, (step, HD))

    each(rows // step, own_scaled)
    dot_sum[...] = jnp.zeros_like(dot_sum)

    def run_norm_back(n):
        d = sum_lo(1, n)
        product = d * scl[:, chunk(n)]
        gp[0, :, chunk(n)] = jnp.sum(product, axis=0, keepdims=True)
        unit = d * gn[:, chunk(n)]
        dn[:, chunk(n)] = unit
        dot_sum[...] += jnp.broadcast_to(
            jnp.sum(unit * scl[:, chunk(n)], axis=1, keepdims=True), dot_sum.shape
        )

    each(NC, run_norm_back)

    def gain_copy(i, to):
        return pltpu.make_async_remote_copy(
            src_ref=gp.at[i], dst_ref=gr.at[i], send_sem=gp_sem.at[2 * i],
            recv_sem=gp_sem.at[2 * i + 1], device_id=to, device_id_type=MESH,
        )

    gain_copy(0, p_core).start()

    def send_back(n):
        mean = dot_sum[:, :1] * (1.0 / width)
        dz = g[block(t), chunk(n)].astype(jnp.float32) + inv[:, :1] * (
            dn[:, chunk(n)] - scl[:, chunk(n)] * mean
        )
        dz = jnp.where(s == 0, jnp.zeros_like(dz), dz)
        hop[1, :, chunk(n)] = dz.astype(jnp.bfloat16)
        hop_copy(1, n, t).start()

    each(NC, send_back)
    gain_copy(0, p_core).wait_recv()
    gp[1] = gp[0] + gr[0]
    gain_copy(1, p_lo).start()

    def run_tail(n):
        spread(1, n)

        @pl.when(n > 1)
        def _():
            forward(1, n - 2)

    each(NC, run_tail)
    forward(1, NC - 2)
    forward(1, NC - 1)
    gain_copy(1, p_lo).wait_recv()
    gp[2] = gp[1] + gr[1]
    gain_out = pltpu.make_async_copy(gp.at[2], out_g, loc_sem.at[0])
    gain_out.start()

    def drain(n):
        collect(0, n)
        collect(1, n)
        st_m(n, t).wait_send()
        st_c(n, t_lo).wait_send()
        st_l(n, t_lo).wait_send()
        st_f(n, t).wait_send()
        for f in range(2):
            rs_core(f, n).wait_send()
            rs_lo(f, n).wait_send()
            hop_copy(f, n, t).wait_send()
            ag(f, n, AG_L, came[f], p_lo).wait_send()
            ag(f, n, AG_C, came[f], p_core).wait_send()
            ag(f, n, AG_F, flip_lo(came[f]), p_core).wait_send()

    each(NC, drain)
    evicted.wait()
    gain_copy(0, p_core).wait_send()
    gain_copy(1, p_lo).wait_send()
    gain_out.wait()


def shards(sections, arrivals, grads_in, stash, gain, w_query, w_key, w_value, w_out):
    _, tokens, width = arrivals.shape
    nq = w_query.shape[2]
    heads = nq // HD
    rows = tokens // 4
    nw = nq + 2 * HD
    cw = width // NC
    f32, bf16 = jnp.float32, jnp.bfloat16
    scratch = [
        pltpu.VMEM((width, nw), bf16),
        pltpu.VMEM((nq, width), bf16),
        pltpu.VMEM((tokens, width), bf16),
        pltpu.VMEM((tokens, width), bf16),
        pltpu.VMEM((tokens, width), bf16),
        pltpu.VMEM((tokens, width), bf16),
        pltpu.VMEM((tokens, nw), bf16),
        pltpu.VMEM((tokens, nq), bf16),
        pltpu.VMEM((tokens, nq), bf16),
        pltpu.VMEM((tokens, nw), bf16),
        pltpu.VMEM((2 * rows, width), f32),
        pltpu.VMEM((tokens, HD), f32),
        pltpu.VMEM((tokens, HD), f32),
        pltpu.VMEM((1, width), f32),
        pltpu.VMEM((2, tokens, HD), f32),
        pltpu.VMEM((rows, width), f32),
        pltpu.VMEM((rows, HD), f32),
        pltpu.VMEM((rows, width), f32),
        pltpu.VMEM((rows, HD), f32),
        pltpu.VMEM((2, NC, 2 * rows, cw), bf16),
        pltpu.VMEM((2, NC, 2 * rows, cw), bf16),
        pltpu.VMEM((2, NC, rows, cw), bf16),
        pltpu.VMEM((2, NC, rows, cw), bf16),
        pltpu.VMEM((2, rows, width), bf16),
        pltpu.VMEM((3, 1, width), f32),
        pltpu.VMEM((2, 1, width), f32),
        pltpu.SemaphoreType.DMA((7 + nq // 256,)),
        pltpu.SemaphoreType.DMA((KINDS, NC)),
        pltpu.SemaphoreType.DMA((KINDS, NC)),
        pltpu.SemaphoreType.DMA((2,)),
        pltpu.SemaphoreType.DMA((4,)),
    ]
    any_spec = pl.BlockSpec(memory_space=pl.ANY)
    flops = 2 * tokens * width * (2 * nw + 2 * nq + nw)
    outs = pl.pallas_call(
        functools.partial(kernel, sections, tokens, width, heads),
        out_shape=(
            jax.ShapeDtypeStruct((1, tokens, width), bf16),
            jax.ShapeDtypeStruct((1, tokens, width), bf16),
            jax.ShapeDtypeStruct((1, rows, width), bf16),
            jax.ShapeDtypeStruct((1, width), f32),
        ),
        in_specs=[any_spec] * 9,
        out_specs=(any_spec,) * 4,
        scratch_shapes=scratch,
        compiler_params=pltpu.CompilerParams(
            collective_id=0, has_side_effects=True, vmem_limit_bytes=60 * 1024 * 1024
        ),
        cost_estimate=pl.CostEstimate(
            flops=flops, bytes_accessed=2 * width * (2 * nw + 6 * tokens), transcendentals=0
        ),
    )(arrivals, grads_in, stash, gain, w_query, w_key, w_value, w_out, jnp.asarray(rope_tables(tokens)))
    return outs


def solution(mesh):
    in_specs = (
        P("section", None, None),
        P("section", None, None),
        P("section", "tp", None),
        P("section", None),
        P("section", None, "tp"),
        P("section", None, "tp"),
        P("section", None, "tp"),
        P("section", "tp", None),
    )
    out_specs = (
        P("section", None, None),
        P("section", None, None),
        P("section", "tp", None),
        P("section", None),
    )
    body = functools.partial(shards, mesh.shape["section"])
    return jax.shard_map(body, mesh=mesh, in_specs=in_specs, out_specs=out_specs, check_vma=False)
```

time: 632 us -> 96.9 us (0.15); the launches traced: 621 us -> 96.8 us
  waiting for transfers between devices: 496 us -> 0 us
  Pallas kernels: 0 us -> 90 us
  matrix products: 51.2 us -> 0 us
  other arithmetic: 20.4 us -> 0 us
  local copies, waits for them, and re-layouts: 22.9 us -> 6.05 us
  starting transfers between devices: 16.1 us -> 0 us
  between operations: 14.4 us -> 0.65 us
    ppermute x7 -> x0, waiting for transfers between devices: 299 us -> none  [the longest x5 255 us: swapped(): return lax.ppermute(value, axis, pairs)]
    psum x1 -> x0, waiting for transfers between devices: 163 us -> none  [shards(): lax.psum(jnp.dot(context, out_w, preferred_element_type=jnp.float32), 'tp')]
    pallas_call x0 -> x1, Pallas kernels: none -> 90 us  [shards(): pl.pallas_call(functools.partial(kernel, sections, tokens, width, heads),...]
    dot_general x15 -> x0, matrix products: 51.2 us -> none  [the longest x4 22.8 us: transposed(): lax.dot_general(left, weight, (((1,), (1,)), ((), ())), preferred_element...]
    all_gather x1 -> x0, waiting for transfers between devices: 33.4 us -> none  [shards(): assembled = lax.all_gather(held, 'tp', axis=0, tiled=True)]
    ppermute x7 -> x0, starting transfers between devices: 16 us -> none  [the longest x5 10.6 us: swapped(): return lax.ppermute(value, axis, pairs)]
    dot_general x1 -> x0, local copies, waits for them, and re-layouts: 11.5 us -> none  [project(): jnp.dot(normed, w_query, preferred_element_type=jnp.float32)]
    reduce_sum x5 -> x0, other arithmetic: 7.02 us -> none  [the longest x1 4.85 us: norm_back(): d_gain = jnp.sum(d_normed * scaled, axis=0)]
  transfers between devices with their start and end apart: 9 -> 0, of which waited for: 9 -> 0; matrix products, arithmetic and copies ran while one was open for 4% -> 0% of each run, Pallas kernels for 0% -> 0%
where the time goes in v1:
time: 96.9 us; the launch traced here: 96.8 us
  Pallas kernels  90 us (93%)
  local copies, waits for them, and re-layouts  6.05 us (6%)
    pallas_call x1, Pallas kernels, shards(): pl.pallas_call(functools.partial(kernel, sections, tokens, width, heads),...  90 us
    unnamed x10, local copies, waits for them, and re-layouts  6.05 us

profile of v1, /device:TPU:1, one launch (start us, length us, event | category | flops | bytes accessed | tf_op | source)
XLA Modules:
  0.0 96.8 jit_solution(5599466624789432266)
XLA Ops:
  0.6 90.0 %shard_map.120 = (bf16[1,256,4096]{2,1,0:T(8,128)(2,1)}, bf16[1,256,4096]{2,1,0:T(8,128)(2,1)}, bf16[1,64,4096]{2,1,0:T(8,128)(2,1)}, f32[1,4096]{1,0:T(1,128)}) custom-call(bf16[1,256,4096]{2,1,0:T(8,128)(2,1)} %arr.1, bf16[1,256,4096]{2,1,0:T(8,128)(2,1)} %grd.1, bf16[1,64,4096]{2,1,0:T(8,128)(2,1)} %sth.1, f32[1,4096]{1,0:T(1,128)} %gain.1, ...), custom_call_target="tpu_custom_call" | custom-call | flops 12348030976 | bytes 33554432 | tf_op jit(solution)/shard_map/pallas_call | solution.py:487
  90.7 0.0 copy-start
  90.7 3.3 %copy.17 = bf16[1,256,4096]{2,1,0:T(8,128)(2,1)} copy(bf16[1,256,4096]{2,1,0:T(8,128)(2,1)} %get-tuple-element.8) | data formatting | bytes 4194304
  94.0 0.0 copy-done
  94.0 0.0 copy-start.1
  94.0 0.0 copy-start.2
  94.0 1.3 %copy.18 = bf16[1,256,4096]{2,1,0:T(8,128)(2,1)} copy(bf16[1,256,4096]{2,1,0:T(8,128)(2,1)S(1)} %copy-done) | data formatting | bytes 4194304
  95.3 0.1 copy-done.1
  95.4 0.8 copy.19
  96.1 0.0 copy-done.2
  96.1 0.6 copy.20
Async XLA Ops:
  90.7 3.3 %copy-start = (bf16[1,256,4096]{2,1,0:T(8,128)(2,1)S(1)}, bf16[1,256,4096]{2,1,0:T(8,128)(2,1)}, u32[]{:S(2)}) copy-start(bf16[1,256,4096]{2,1,0:T(8,128)(2,1)} %get-tuple-element.9) | copy-start | bytes 6291460
  94.0 1.4 %copy-start.1 = (bf16[1,64,4096]{2,1,0:T(8,128)(2,1)S(1)}, bf16[1,64,4096]{2,1,0:T(8,128)(2,1)}, u32[]{:S(2)}) copy-start(bf16[1,64,4096]{2,1,0:T(8,128)(2,1)} %get-tuple-element.10) | copy-start | bytes 1572868
  94.0 2.2 %copy-start.2 = (f32[1,4096]{1,0:T(1,128)S(1)}, f32[1,4096]{1,0:T(1,128)}, u32[]{:S(2)}) copy-start(f32[1,4096]{1,0:T(1,128)} %get-tuple-element.11) | copy-start | bytes 49156

commit v2 on v1

--- a/solution.py
+++ b/solution.py
@@ -9,7 +9,10 @@
 from jax.sharding import PartitionSpec as P
 
 HD = 128
+LOG2E = 1.4426950408889634
 NC = 8
+PAIR = 2
+NH = NC // 2
 EPSILON = 1e-05
 MESH = pl.DeviceIdType.MESH
 NN = (((1,), (0,)), ((), ()))
@@ -41,7 +44,7 @@
     arr, grd, sth, gain, wq, wk, wv, wo, rope,
     out_f, out_b, evict, out_g,
     w, wob, zf, g, zb, nrm, qkv, ctx, dctx, dqkv, mine, dk, dv, gn, rp, scl, inv, dn, dot_sum,
-    sc, rc, sl, rl, hop, gp, gr,
+    sc_f, rc_f, sl_f, rl_f, sc_b, rc_b, sl_b, rl_b, hop, gp, gr,
     loc_sem, send_sem, recv_sem, ev_sem, gp_sem,
 ):
     nq = heads * HD
@@ -97,34 +100,32 @@
     loads[0].start()
     loads[1].start()
     loads[4].start()
+
+    barrier = pltpu.get_barrier_semaphore()
+    for device in (p_core, p_lo, p_mir, p_next, p_prev):
+        pl.semaphore_signal(barrier, inc=1, device_id=device, device_id_type=MESH)
+    pl.semaphore_wait(barrier, 5)
+
+    def st_m(n, at):
+        return remote(sth.at[0, :, chunk(n)], zb.at[block(at), chunk(n)], ST_M, n, p_mir)
+
+    def st_c(n, at):
+        return remote(zb.at[block(t_lo), chunk(n)], zb.at[block(at), chunk(n)], ST_C, n, p_core)
+
+    def st_l(n, at):
+        return remote(zb.at[block(t_lo), chunk(n)], zb.at[block(at), chunk(n)], ST_L, n, p_lo)
+
+    def st_f(n, at):
+        return remote(zb.at[block(t), chunk(n)], zb.at[block(at), chunk(n)], ST_F, n, p_core)
+
+    def each(count, body):
+        lax.fori_loop(0, count, lambda i, c: (body(i), c)[1], 0)
+
+    each(NC, lambda n: st_m(n, t).start())
     for n in range(tiles):
         load_q(n).start()
     loads[2].start()
     loads[3].start()
-    loads[5].start()
-    loads[6].start()
-
-    barrier = pltpu.get_barrier_semaphore()
-    for device in (p_core, p_lo, p_mir, p_next, p_prev):
-        pl.semaphore_signal(barrier, inc=1, device_id=device, device_id_type=MESH)
-    pl.semaphore_wait(barrier, 5)
-
-    def st_m(n, at):
-        return remote(sth.at[0, :, chunk(n)], zb.at[block(at), chunk(n)], ST_M, n, p_mir)
-
-    def st_c(n, at):
-        return remote(zb.at[block(t_lo), chunk(n)], zb.at[block(at), chunk(n)], ST_C, n, p_core)
-
-    def st_l(n, at):
-        return remote(zb.at[block(t_lo), chunk(n)], zb.at[block(at), chunk(n)], ST_L, n, p_lo)
-
-    def st_f(n, at):
-        return remote(zb.at[block(t), chunk(n)], zb.at[block(at), chunk(n)], ST_F, n, p_core)
-
-    def each(count, body):
-        lax.fori_loop(0, count, lambda i, c: (body(i), c)[1], 0)
-
-    each(NC, lambda n: st_m(n, t).start())
 
     def stash_spread(n):
         st_m(n, t_lo).wait_recv()
@@ -143,6 +144,8 @@
         src_ref=arr.at[0, block(t_lo)], dst_ref=evict.at[0], send_sem=ev_sem.at[0],
         recv_sem=ev_sem.at[1], device_id=p_mir, device_id_type=MESH,
     )
+
+    evicted.start()
 
     step = 16
 
@@ -175,80 +178,132 @@
     def place(b):
         low = (b % 2 + t % 2) % 2
         high = (b // 2 + t // 2) % 2
-        return block(2 * low + high)
-
-    def put(ref, cols, value):
+        return 2 * low + high
+
+    def put(cols, value):
         for b in range(4):
-            ref[place(b), cols] = value[b * rows:(b + 1) * rows]
+            ctx[block(place(b)), cols] = value[b * rows:(b + 1) * rows]
+
+    def put_back(cols, value):
+        part = rows // 2
+        for b in range(4):
+            for half in range(2):
+                at = place(b)
+                at = (at // 2) * 2 * rows + half * rows + (at % 2) * part
+                to = pl.ds(pl.multiple_of(at, part), part)
+                dqkv[to, cols] = value[b * rows + half * part:b * rows + (half + 1) * part]
 
     def head_cols(h):
         return pl.ds(pl.multiple_of(h * HD, HD), HD)
 
     scale = HD ** (-0.5)
+    mid = tokens // 2
+    bfloat = jnp.bfloat16
+
+    def softmax(scores, axis):
+        highest = jnp.max(scores, axis=axis, keepdims=True)
+        e = jnp.exp2((scores - highest) * (scale * LOG2E))
+        return e * (1.0 / jnp.sum(e, axis=axis, keepdims=True))
+
+    def causal(scores, q_axis):
+        q_at = lax.broadcasted_iota(jnp.int32, scores.shape, q_axis)
+        k_at = lax.broadcasted_iota(jnp.int32, scores.shape, 1 - q_axis)
+        return jnp.where(q_at >= k_at, scores, -jnp.inf)
 
     def attend(h):
         cols = head_cols(h)
-        scores = dot(qkv[:, cols], qkv[:, nq:nq + HD], NT) * scale
-        q_at = lax.broadcasted_iota(jnp.int32, scores.shape, 0)
-        k_at = lax.broadcasted_iota(jnp.int32, scores.shape, 1)
-        scores = jnp.where(q_at >= k_at, scores, -jnp.inf)
-        e = jnp.exp(scores - jnp.max(scores, axis=1, keepdims=True))
-        probs = e / jnp.sum(e, axis=1, keepdims=True)
-        out = dot(probs.astype(jnp.bfloat16), qkv[:, nq + HD:])
-        put(ctx, cols, out.astype(jnp.bfloat16))
+        q, k, v = qkv[:, cols], qkv[:, nq:nq + HD], qkv[:, nq + HD:]
+        early = softmax(causal(dot(q[:mid], k[:mid], NT), 0), 1)
+        late = dot(q[mid:], k, NT)
+        late = softmax(jnp.concatenate([late[:, :mid], causal(late[:, mid:], 0)], axis=1), 1)
+        out = jnp.concatenate(
+            [dot(early.astype(bfloat), v[:mid]), dot(late.astype(bfloat), v)], axis=0
+        )
+        put(cols, out.astype(bfloat))
 
     def attend_back(h):
         cols = head_cols(h)
         q, k, v = qkv[:, cols], qkv[:, nq:nq + HD], qkv[:, nq + HD:]
         dc = dctx[:, cols]
-        scores = dot(k, q, NT) * scale
-        k_at = lax.broadcasted_iota(jnp.int32, scores.shape, 0)
-        q_at = lax.broadcasted_iota(jnp.int32, scores.shape, 1)
-        scores = jnp.where(q_at >= k_at, scores, -jnp.inf)
-        e = jnp.exp(scores - jnp.max(scores, axis=0, keepdims=True))
-        probs = e / jnp.sum(e, axis=0, keepdims=True)
-        d_probs = dot(v, dc, NT)
-        inner = jnp.sum(probs * d_probs, axis=0, keepdims=True)
-        d_scores = (probs * (d_probs - inner) * scale).astype(jnp.bfloat16)
+
+        def half(scores, d_probs):
+            probs = softmax(scores, 0)
+            inner = jnp.sum(probs * d_probs, axis=0, keepdims=True)
+            return probs.astype(bfloat), (probs * (d_probs - inner) * scale).astype(bfloat)
+
+        p_early, s_early = half(causal(dot(k[:mid], q[:mid], NT), 1), dot(v[:mid], dc[:mid], NT))
+        late = dot(k, q[mid:], NT)
+        late = jnp.concatenate([late[:mid], causal(late[mid:], 1)], axis=0)
+        p_late, s_late = half(late, dot(v, dc[mid:], NT))
+
+        def whole(first, second):
+            first = jnp.concatenate([first, jnp.zeros_like(first)], axis=0)
+            return jnp.concatenate([first, second], axis=1)
+
+        d_scores = whole(s_early, s_late)
         dk[...] += dot(d_scores, q)
-        dv[...] += dot(probs.astype(jnp.bfloat16), dc)
-        put(dqkv, cols, turn(dot(d_scores, k, TN), -1.0).astype(jnp.bfloat16))
+        dv[...] += dot(whole(p_early, p_late), dc)
+        put_back(cols, turn(dot(d_scores, k, TN), -1.0).astype(bfloat))
 
     def context_back(n):
         cols = pl.ds(pl.multiple_of(n * tile, tile), tile)
         dctx[:, cols] = dot(g[...], wob[cols, :], NT).astype(jnp.bfloat16)
 
+    sc, rc, sl, rl = (sc_f, sc_b), (rc_f, rc_b), (sl_f, sl_b), (rl_f, rl_b)
+
+    def extent(f, n):
+        if f == 0:
+            return 0, rows, chunk(n), 0
+        half = n // NH
+        cols = pl.ds(pl.multiple_of((n % NH) * (width // NH), width // NH), width // NH)
+        first = pl.multiple_of(half * (rows // 2), rows // 2)
+        return first, rows // 2, cols, pl.multiple_of(half * rows, rows)
+
     def rs_core(f, n):
-        return remote(sc.at[f, n], rc.at[f, n], RS_C + PASS * f, n, p_core)
+        return remote(sc[f].at[n], rc[f].at[n], RS_C + PASS * f, n, p_core)
 
     def rs_lo(f, n):
-        return remote(sl.at[f, n], rl.at[f, n], RS_L + PASS * f, n, p_lo)
+        return remote(sl[f].at[n], rl[f].at[n], RS_L + PASS * f, n, p_lo)
 
     def sum_send(f, n, part):
-        sc[f, n] = part[2 * rows:].astype(jnp.bfloat16)
+        sc[f][n] = part[2 * rows:].astype(jnp.bfloat16)
         rs_core(f, n).start()
         mine[:, chunk(n)] = part[:2 * rows]
 
-    def sum_core(f, n):
-        rs_core(f, n).wait_recv()
-        total = mine[:, chunk(n)] + rc[f, n].astype(jnp.float32)
-        sl[f, n] = total[rows:].astype(jnp.bfloat16)
-        rs_lo(f, n).start()
+    def sum_core(n):
+        rs_core(0, n).wait_recv()
+        total = mine[:, chunk(n)] + rc_f[n].astype(jnp.float32)
+        sl_f[n] = total[rows:].astype(jnp.bfloat16)
+        rs_lo(0, n).start()
         mine[:rows, chunk(n)] = total[:rows]
 
+    def sum_core_back(n):
+        rs_core(1, n).wait_recv()
+        total = mine[:, chunk(n)] + rc_b[n].astype(jnp.float32)
+        part = rows // 2
+        cols = pl.ds(pl.multiple_of((n % 2) * cw, cw), cw)
+        for half in range(2):
+            at = half * rows
+            sl_b[half * NH + n // 2, :, cols] = total[at + part:at + rows].astype(jnp.bfloat16)
+            mine[at:at + part, chunk(n)] = total[at:at + part]
+
     def sum_lo(f, n):
+        _, count, cols, at = extent(f, n)
         rs_lo(f, n).wait_recv()
-        return mine[:rows, chunk(n)] + rl[f, n].astype(jnp.float32)
+        return mine[pl.ds(at, count), cols] + rl[f][n].astype(jnp.float32)
 
     outs = (out_f, out_b)
     hops = (p_next, p_prev)
     came = ((t + 2 * first_z) % 4, (t + 2 * last_z) % 4)
 
     def at_out(f, b, n):
-        return outs[f].at[0, block(b), chunk(n)]
+        first, count, cols, _ = extent(f, n)
+        return outs[f].at[0, pl.ds(pl.multiple_of(b * rows + first, count), count), cols]
 
     def hop_copy(f, n, b):
-        return remote(hop.at[f, :, chunk(n)], at_out(f, b, n), HOP + PASS * f, n, hops[f])
+        first, count, cols, _ = extent(f, n)
+        src = hop.at[f, pl.ds(first, count), cols]
+        return remote(src, at_out(f, b, n), HOP + PASS * f, n, hops[f])
 
     def ag(f, n, kind, b, to):
         return remote(at_out(f, b, n), at_out(f, b, n), kind + PASS * f, n, to)
@@ -275,88 +330,110 @@
         ag(f, n, AG_C, b, p_core).wait_recv()
         ag(f, n, AG_F, flip_lo(b), p_core).wait_recv()
 
+    def spread_f(n):
+        spread(0, n)
+
+    def forward_f(n):
+        forward(0, n)
+
     def finish_f(n):
         y = zf[block(t), chunk(n)].astype(jnp.float32) + sum_lo(0, n)
         y = jnp.where(s == sections - 1, jnp.zeros_like(y), y)
         hop[0, :, chunk(n)] = y.astype(jnp.bfloat16)
         hop_copy(0, n, t).start()
 
+    def loop(count, body, after):
+        def both(i):
+            body(i)
+            for at, steps in after.items():
+
+                @pl.when(i == at)
+                def _():
+                    for act, n in steps:
+                        act(n)
+
+        each(count, both)
+
+    def heads_of(body):
+        def several(i):
+            for k in range(PAIR):
+                body(PAIR * i + k)
+
+        return several
+
     loads[0].wait()
     loads[1].wait()
     normalize(zf)
+    loads[6].start()
+    loads[5].start()
     loads[4].wait()
 
     def run_project(i):
         load_q(i).wait()
         project_q(i)
-        stash_spread(i)
 
     each(tiles, run_project)
     loads[2].wait()
     loads[3].wait()
     project_kv()
+    stash_spread(0)
+    loop(heads // PAIR, heads_of(attend), {i: [(stash_spread, i + 1)] for i in range(4)})
     loads[5].wait()
     loads[6].wait()
-
-    def run_context_back(i):
-        context_back(i)
-        stash_spread(NC - tiles + i)
-
-    each(tiles, run_context_back)
-    evicted.start()
-
-    def run_attend(h):
-        attend(h)
-        stash_forward(h)
-
-    each(heads, run_attend)
+    loop(tiles, context_back, {1: [(stash_spread, 5)], 3: [(stash_spread, 6)]})
 
     def run_out(n):
         sum_send(0, n, dot(ctx[...], wob[:, chunk(n)]))
 
         @pl.when(n > 0)
         def _():
-            sum_core(0, n - 1)
+            sum_core(n - 1)
+
+        @pl.when(n == 2)
+        def _():
+            stash_spread(NC - 1)
+
+        stash_forward(n)
 
     each(NC, run_out)
-    sum_core(0, NC - 1)
-
+    sum_core(NC - 1)
     each(NC, stash_last)
     normalize(zb)
-
-    def run_project_b(i):
-        project_q(i)
-        finish_f(i)
-
-    each(tiles, run_project_b)
+    finish_f(0)
+    finish_f(1)
+    loop(tiles, project_q, {
+        0: [(finish_f, 2)],
+        1: [(finish_f, 3)],
+        2: [(finish_f, 4), (spread_f, 0)],
+        3: [(finish_f, 5), (spread_f, 1)],
+    })
     project_kv()
     dk[...] = jnp.zeros_like(dk)
     dv[...] = jnp.zeros_like(dv)
-
-    def run_attend_back(h):
-        attend_back(h)
-
-        @pl.when(h < NC - tiles)
-        def _():
-            finish_f(tiles + h)
-
-        spread(0, h)
-
-    each(heads, run_attend_back)
-    put(dqkv, pl.ds(nq, HD), turn(dk[...], -1.0).astype(jnp.bfloat16))
-    put(dqkv, pl.ds(nq + HD, HD), dv[...].astype(jnp.bfloat16))
+    loop(heads // PAIR, heads_of(attend_back), {
+        0: [(finish_f, 6), (finish_f, 7), (spread_f, 2)],
+        1: [(spread_f, 3), (spread_f, 4)],
+        2: [(spread_f, 5), (spread_f, 6)],
+        3: [(spread_f, 7)],
+    })
+    put_back(pl.ds(nq, HD), turn(dk[...], -1.0).astype(jnp.bfloat16))
+    put_back(pl.ds(nq + HD, HD), dv[...].astype(jnp.bfloat16))
 
     def run_d_normed(n):
         sum_send(1, n, dot(dqkv[...], w[chunk(n), :], NT))
 
         @pl.when(n > 0)
         def _():
-            sum_core(1, n - 1)
-
-        forward(0, n)
+            sum_core_back(n - 1)
+
+            @pl.when(n % 2 == 0)
+            def _():
+                rs_lo(1, n // 2 - 1).start()
 
     each(NC, run_d_normed)
-    sum_core(1, NC - 1)
+    sum_core_back(NC - 1)
+    for n in range(NH - 1, NC):
+        rs_lo(1, n).start()
 
     def own_scaled(i):
         at = pl.ds(pl.multiple_of(t * rows + i * step, step), step)
@@ -369,18 +446,18 @@
 
     each(rows // step, own_scaled)
     dot_sum[...] = jnp.zeros_like(dot_sum)
+    gp[0] = jnp.zeros((1, width), jnp.float32)
+    each(NC, forward_f)
 
     def run_norm_back(n):
+        first, count, cols, _ = extent(1, n)
+        at = pl.ds(first, count)
         d = sum_lo(1, n)
-        product = d * scl[:, chunk(n)]
-        gp[0, :, chunk(n)] = jnp.sum(product, axis=0, keepdims=True)
-        unit = d * gn[:, chunk(n)]
-        dn[:, chunk(n)] = unit
-        dot_sum[...] += jnp.broadcast_to(
-            jnp.sum(unit * scl[:, chunk(n)], axis=1, keepdims=True), dot_sum.shape
-        )
-
-    each(NC, run_norm_back)
+        scaled = scl[at, cols]
+        gp[0, :, cols] += jnp.sum(d * scaled, axis=0, keepdims=True)
+        unit = d * gn[:, cols]
+        dn[at, cols] = unit
+        dot_sum[at] += jnp.broadcast_to(jnp.sum(unit * scaled, axis=1, keepdims=True), (count, HD))
 
     def gain_copy(i, to):
         return pltpu.make_async_remote_copy(
@@ -388,30 +465,33 @@
             recv_sem=gp_sem.at[2 * i + 1], device_id=to, device_id_type=MESH,
         )
 
+    def send_back(n):
+        first, count, cols, _ = extent(1, n)
+        at = pl.ds(first, count)
+        mean = dot_sum[at, :1] * (1.0 / width)
+        upstream = g[pl.ds(pl.multiple_of(t * rows + first, count), count), cols]
+        dz = upstream.astype(jnp.float32) + inv[at, :1] * (dn[at, cols] - scl[at, cols] * mean)
+        dz = jnp.where(s == 0, jnp.zeros_like(dz), dz)
+        hop[1, at, cols] = dz.astype(jnp.bfloat16)
+        hop_copy(1, n, t).start()
+
+    each(NH, run_norm_back)
+    each(NH, send_back)
+    spread(1, 0)
+    spread(1, 1)
+    each(NH, lambda n: run_norm_back(n + NH))
+    each(NH, lambda n: send_back(n + NH))
     gain_copy(0, p_core).start()
 
-    def send_back(n):
-        mean = dot_sum[:, :1] * (1.0 / width)
-        dz = g[block(t), chunk(n)].astype(jnp.float32) + inv[:, :1] * (
-            dn[:, chunk(n)] - scl[:, chunk(n)] * mean
-        )
-        dz = jnp.where(s == 0, jnp.zeros_like(dz), dz)
-        hop[1, :, chunk(n)] = dz.astype(jnp.bfloat16)
-        hop_copy(1, n, t).start()
-
-    each(NC, send_back)
+    def run_tail(n):
+        spread(1, n + 2)
+        forward(1, n)
+
+    each(2, run_tail)
     gain_copy(0, p_core).wait_recv()
     gp[1] = gp[0] + gr[0]
     gain_copy(1, p_lo).start()
-
-    def run_tail(n):
-        spread(1, n)
-
-        @pl.when(n > 1)
-        def _():
-            forward(1, n - 2)
-
-    each(NC, run_tail)
+    each(NC - 4, lambda n: run_tail(n + 2))
     forward(1, NC - 2)
     forward(1, NC - 1)
     gain_copy(1, p_lo).wait_recv()
@@ -439,6 +519,19 @@
     gain_copy(0, p_core).wait_send()
     gain_copy(1, p_lo).wait_send()
     gain_out.wait()
+
+
+def store(f, b, e, g, to_f, to_b, to_e, to_g, sem):
+    copies = [pltpu.make_async_copy(g, to_g, sem.at[3, 0])]
+    for i, (src, dst) in enumerate(((f, to_f), (b, to_b), (e, to_e))):
+        part = src.shape[1] // 4
+        for k in range(4):
+            at = pl.ds(k * part, part)
+            copies.append(pltpu.make_async_copy(src.at[0, at], dst.at[0, at], sem.at[i, k]))
+    for copy in copies:
+        copy.start()
+    for copy in copies:
+        copy.wait()
 
 
 def shards(sections, arrivals, grads_in, stash, gain, w_query, w_key, w_value, w_out):
@@ -469,10 +562,14 @@
         pltpu.VMEM((rows, HD), f32),
         pltpu.VMEM((rows, width), f32),
         pltpu.VMEM((rows, HD), f32),
-        pltpu.VMEM((2, NC, 2 * rows, cw), bf16),
-        pltpu.VMEM((2, NC, 2 * rows, cw), bf16),
-        pltpu.VMEM((2, NC, rows, cw), bf16),
-        pltpu.VMEM((2, NC, rows, cw), bf16),
+        pltpu.VMEM((NC, 2 * rows, cw), bf16),
+        pltpu.VMEM((NC, 2 * rows, cw), bf16),
+        pltpu.VMEM((NC, rows, cw), bf16),
+        pltpu.VMEM((NC, rows, cw), bf16),
+        pltpu.VMEM((NC, 2 * rows, cw), bf16),
+        pltpu.VMEM((NC, 2 * rows, cw), bf16),
+        pltpu.VMEM((NC, rows // 2, 2 * cw), bf16),
+        pltpu.VMEM((NC, rows // 2, 2 * cw), bf16),
         pltpu.VMEM((2, rows, width), bf16),
         pltpu.VMEM((3, 1, width), f32),
         pltpu.VMEM((2, 1, width), f32),
@@ -483,26 +580,35 @@
         pltpu.SemaphoreType.DMA((4,)),
     ]
     any_spec = pl.BlockSpec(memory_space=pl.ANY)
+    results = (
+        jax.ShapeDtypeStruct((1, tokens, width), bf16),
+        jax.ShapeDtypeStruct((1, tokens, width), bf16),
+        jax.ShapeDtypeStruct((1, rows, width), bf16),
+        jax.ShapeDtypeStruct((1, width), f32),
+    )
     flops = 2 * tokens * width * (2 * nw + 2 * nq + nw)
     outs = pl.pallas_call(
         functools.partial(kernel, sections, tokens, width, heads),
-        out_shape=(
-            jax.ShapeDtypeStruct((1, tokens, width), bf16),
-            jax.ShapeDtypeStruct((1, tokens, width), bf16),
-            jax.ShapeDtypeStruct((1, rows, width), bf16),
-            jax.ShapeDtypeStruct((1, width), f32),
-        ),
+        out_shape=tuple(pltpu.VMEM(r.shape, r.dtype) for r in results),
         in_specs=[any_spec] * 9,
         out_specs=(any_spec,) * 4,
         scratch_shapes=scratch,
         compiler_params=pltpu.CompilerParams(
-            collective_id=0, has_side_effects=True, vmem_limit_bytes=60 * 1024 * 1024
+            collective_id=0, has_side_effects=True, vmem_limit_bytes=50 * 1024 * 1024
         ),
         cost_estimate=pl.CostEstimate(
             flops=flops, bytes_accessed=2 * width * (2 * nw + 6 * tokens), transcendentals=0
         ),
     )(arrivals, grads_in, stash, gain, w_query, w_key, w_value, w_out, jnp.asarray(rope_tables(tokens)))
-    return outs
+    return pl.pallas_call(
+        store,
+        out_shape=tuple(pltpu.HBM(r.shape, r.dtype) for r in results),
+        in_specs=[any_spec] * 4,
+        out_specs=(any_spec,) * 4,
+        scratch_shapes=[pltpu.SemaphoreType.DMA((4, 4))],
+        compiler_params=pltpu.CompilerParams(vmem_limit_bytes=1024 * 1024),
+        cost_estimate=pl.CostEstimate(flops=0, bytes_accessed=18 * tokens * width, transcendentals=0),
+    )(*outs)
 
 
 def solution(mesh):

time: 96.9 us -> 86.6 us (0.89)
  local copies, waits for them, and re-layouts: 6.05 us -> 0 us
  Pallas kernels: 90 us -> 85.9 us
    pallas_call x1, Pallas kernels: 90 us -> 83.6 us  [shards(): pl.pallas_call(functools.partial(kernel, sections, tokens, width, heads),...]
    unnamed x10 -> x0, local copies, waits for them, and re-layouts: 6.05 us -> none
    pallas_call x0 -> x1, Pallas kernels: none -> 2.3 us  [shards(): pl.pallas_call(store, out_shape=tuple((pltpu.HBM(r.shape, r.dtype) for r...]
where the time goes in v2:
time: 86.6 us; the launch traced here: 86.5 us
  Pallas kernels  85.9 us (99%)
    pallas_call x1, Pallas kernels, shards(): pl.pallas_call(functools.partial(kernel, sections, tokens, width, heads),...  83.6 us
    pallas_call x1, Pallas kernels, shards(): pl.pallas_call(store, out_shape=tuple((pltpu.HBM(r.shape, r.dtype) for r...  2.3 us

profile of v2, /device:TPU:1, one launch (start us, length us, event | category | flops | bytes accessed | tf_op | source)
XLA Modules:
  0.0 86.5 jit_solution(16335955338849120601)
XLA Ops:
  0.6 83.6 %shard_map.120 = (bf16[1,256,4096]{2,1,0:T(8,128)(2,1)S(1)}, bf16[1,256,4096]{2,1,0:T(8,128)(2,1)S(1)}, bf16[1,64,4096]{2,1,0:T(8,128)(2,1)S(1)}, f32[1,4096]{1,0:T(1,128)S(1)}) custom-call(bf16[1,256,4096]{2,1,0:T(8,128)(2,1)} %arr.1, bf16[1,256,4096]{2,1,0:T(8,128)(2,1)} %grd.1, bf16[1,64,4096]{2,1,0:T(8,128)(2,1)} %sth.1, f32[1,4096]{1,0:T(1,128)} %gain.1, ...), custom_call_target="tpu_custom_call" | custom-call | flops 12348030976 | bytes 33554432 | tf_op jit(solution)/shard_map/pallas_call | solution.py:590
  84.2 2.3 %shard_map.121 = (bf16[1,256,4096]{2,1,0:T(8,128)(2,1)}, bf16[1,256,4096]{2,1,0:T(8,128)(2,1)}, bf16[1,64,4096]{2,1,0:T(8,128)(2,1)}, f32[1,4096]{1,0:T(1,128)}) custom-call(bf16[1,256,4096]{2,1,0:T(8,128)(2,1)S(1)} %get-tuple-element.8.f, bf16[1,256,4096]{2,1,0:T(8,128)(2,1)S(1)} %get-tuple-element.9.b, bf16[1,64,4096]{2,1,0:T(8,128)(2,1)S(1)} %get-tuple-element.10.e, ...), custom_call_target="tpu_custom_call" | custom-call | bytes 18874368 | tf_op jit(solution)/shard_map/pallas_call | solution.py:603

commit v3 on v2

--- a/solution.py
+++ b/solution.py
@@ -11,7 +11,8 @@
 HD = 128
 LOG2E = 1.4426950408889634
 NC = 8
-PAIR = 2
+EARLY = 3
+PAIR = 4
 NH = NC // 2
 EPSILON = 1e-05
 MESH = pl.DeviceIdType.MESH
@@ -64,6 +65,8 @@
     p_mir = (sections - 1 - s, t_lo)
     p_next = ((s + 1) % sections, t_next)
     p_prev = ((s + sections - 1) % sections, t_prev)
+    p_next_lo = ((s + 1) % sections, (t_next + 2) % 4)
+    p_prev_lo = ((s + sections - 1) % sections, (t_prev + 2) % 4)
 
     def block(index):
         return pl.ds(pl.multiple_of(index * rows, rows), rows)
@@ -100,32 +103,32 @@
     loads[0].start()
     loads[1].start()
     loads[4].start()
-
-    barrier = pltpu.get_barrier_semaphore()
-    for device in (p_core, p_lo, p_mir, p_next, p_prev):
-        pl.semaphore_signal(barrier, inc=1, device_id=device, device_id_type=MESH)
-    pl.semaphore_wait(barrier, 5)
-
-    def st_m(n, at):
-        return remote(sth.at[0, :, chunk(n)], zb.at[block(at), chunk(n)], ST_M, n, p_mir)
-
-    def st_c(n, at):
-        return remote(zb.at[block(t_lo), chunk(n)], zb.at[block(at), chunk(n)], ST_C, n, p_core)
-
-    def st_l(n, at):
-        return remote(zb.at[block(t_lo), chunk(n)], zb.at[block(at), chunk(n)], ST_L, n, p_lo)
-
-    def st_f(n, at):
-        return remote(zb.at[block(t), chunk(n)], zb.at[block(at), chunk(n)], ST_F, n, p_core)
-
-    def each(count, body):
-        lax.fori_loop(0, count, lambda i, c: (body(i), c)[1], 0)
-
-    each(NC, lambda n: st_m(n, t).start())
     for n in range(tiles):
         load_q(n).start()
     loads[2].start()
     loads[3].start()
+
+    barrier = pltpu.get_barrier_semaphore()
+    for device in (p_core, p_lo, p_mir, p_next, p_prev, p_next_lo, p_prev_lo):
+        pl.semaphore_signal(barrier, inc=1, device_id=device, device_id_type=MESH)
+    pl.semaphore_wait(barrier, 7)
+
+    def st_m(n, at):
+        return remote(sth.at[0, :, chunk(n)], zb.at[block(at), chunk(n)], ST_M, n, p_mir)
+
+    def st_c(n, at):
+        return remote(zb.at[block(t_lo), chunk(n)], zb.at[block(at), chunk(n)], ST_C, n, p_core)
+
+    def st_l(n, at):
+        return remote(zb.at[block(t_lo), chunk(n)], zb.at[block(at), chunk(n)], ST_L, n, p_lo)
+
+    def st_f(n, at):
+        return remote(zb.at[block(t), chunk(n)], zb.at[block(at), chunk(n)], ST_F, n, p_core)
+
+    def each(count, body):
+        lax.fori_loop(0, count, lambda i, c: (body(i), c)[1], 0)
+
+    each(NC, lambda n: st_m(n, t).start())
 
     def stash_spread(n):
         st_m(n, t_lo).wait_recv()
@@ -305,6 +308,10 @@
         src = hop.at[f, pl.ds(first, count), cols]
         return remote(src, at_out(f, b, n), HOP + PASS * f, n, hops[f])
 
+    def far_copy(n, b):
+        src = hop.at[0, :, chunk(n)]
+        return remote(src, at_out(0, b, n), AG_L, n, p_next_lo)
+
     def ag(f, n, kind, b, to):
         return remote(at_out(f, b, n), at_out(f, b, n), kind + PASS * f, n, to)
 
@@ -317,12 +324,16 @@
     def spread(f, n):
         b = came[f]
         hop_copy(f, n, b).wait_recv()
-        ag(f, n, AG_L, b, p_lo).start()
+        if f == 1:
+            ag(f, n, AG_L, b, p_lo).start()
         ag(f, n, AG_C, b, p_core).start()
 
     def forward(f, n):
         b = flip_lo(came[f])
-        ag(f, n, AG_L, b, p_lo).wait_recv()
+        if f == 0:
+            far_copy(n, b).wait_recv()
+        else:
+            ag(f, n, AG_L, b, p_lo).wait_recv()
         ag(f, n, AG_F, b, p_core).start()
 
     def collect(f, n):
@@ -330,10 +341,8 @@
         ag(f, n, AG_C, b, p_core).wait_recv()
         ag(f, n, AG_F, flip_lo(b), p_core).wait_recv()
 
-    def spread_f(n):
+    def settle_f(n):
         spread(0, n)
-
-    def forward_f(n):
         forward(0, n)
 
     def finish_f(n):
@@ -341,6 +350,7 @@
         y = jnp.where(s == sections - 1, jnp.zeros_like(y), y)
         hop[0, :, chunk(n)] = y.astype(jnp.bfloat16)
         hop_copy(0, n, t).start()
+        far_copy(n, t).start()
 
     def loop(count, body, after):
         def both(i):
@@ -377,7 +387,7 @@
     loads[3].wait()
     project_kv()
     stash_spread(0)
-    loop(heads // PAIR, heads_of(attend), {i: [(stash_spread, i + 1)] for i in range(4)})
+    loop(heads // PAIR, heads_of(attend), {i: [(stash_spread, 2 * i + 1), (stash_spread, 2 * i + 2)] for i in range(2)})
     loads[5].wait()
     loads[6].wait()
     loop(tiles, context_back, {1: [(stash_spread, 5)], 3: [(stash_spread, 6)]})
@@ -401,21 +411,12 @@
     normalize(zb)
     finish_f(0)
     finish_f(1)
-    loop(tiles, project_q, {
-        0: [(finish_f, 2)],
-        1: [(finish_f, 3)],
-        2: [(finish_f, 4), (spread_f, 0)],
-        3: [(finish_f, 5), (spread_f, 1)],
-    })
+    loop(tiles, project_q, {i: [(finish_f, i + 2)] for i in range(4)})
     project_kv()
+    finish_f(6)
     dk[...] = jnp.zeros_like(dk)
     dv[...] = jnp.zeros_like(dv)
-    loop(heads // PAIR, heads_of(attend_back), {
-        0: [(finish_f, 6), (finish_f, 7), (spread_f, 2)],
-        1: [(spread_f, 3), (spread_f, 4)],
-        2: [(spread_f, 5), (spread_f, 6)],
-        3: [(spread_f, 7)],
-    })
+    loop(heads // PAIR, heads_of(attend_back), {0: [(finish_f, 7)]})
     put_back(pl.ds(nq, HD), turn(dk[...], -1.0).astype(jnp.bfloat16))
     put_back(pl.ds(nq + HD, HD), dv[...].astype(jnp.bfloat16))
 
@@ -447,7 +448,7 @@
     each(rows // step, own_scaled)
     dot_sum[...] = jnp.zeros_like(dot_sum)
     gp[0] = jnp.zeros((1, width), jnp.float32)
-    each(NC, forward_f)
+    each(EARLY, settle_f)
 
     def run_norm_back(n):
         first, count, cols, _ = extent(1, n)
@@ -488,6 +489,7 @@
         forward(1, n)
 
     each(2, run_tail)
+    each(NC - EARLY, lambda n: settle_f(n + EARLY))
     gain_copy(0, p_core).wait_recv()
     gp[1] = gp[0] + gr[0]
     gain_copy(1, p_lo).start()
@@ -510,7 +512,10 @@
             rs_core(f, n).wait_send()
             rs_lo(f, n).wait_send()
             hop_copy(f, n, t).wait_send()
-            ag(f, n, AG_L, came[f], p_lo).wait_send()
+            if f == 0:
+                far_copy(n, t).wait_send()
+            else:
+                ag(f, n, AG_L, came[f], p_lo).wait_send()
             ag(f, n, AG_C, came[f], p_core).wait_send()
             ag(f, n, AG_F, flip_lo(came[f]), p_core).wait_send()
 

time: 86.6 us -> 81.5 us (0.941)
  Pallas kernels: 85.9 us -> 80.7 us
    pallas_call x1, Pallas kernels: 83.6 us -> 78.4 us  [shards(): pl.pallas_call(functools.partial(kernel, sections, tokens, width, heads),...]
where the time goes in v3:
time: 81.5 us; the launch traced here: 81.4 us
  Pallas kernels  80.7 us (99%)
    pallas_call x1, Pallas kernels, shards(): pl.pallas_call(functools.partial(kernel, sections, tokens, width, heads),...  78.4 us
    pallas_call x1, Pallas kernels, shards(): pl.pallas_call(store, out_shape=tuple((pltpu.HBM(r.shape, r.dtype) for r...  2.3 us

profile of v3, /device:TPU:1, one launch (start us, length us, event | category | flops | bytes accessed | tf_op | source)
XLA Modules:
  0.0 81.4 jit_solution(12518889726745589693)
XLA Ops:
  0.6 78.4 %shard_map.120 = (bf16[1,256,4096]{2,1,0:T(8,128)(2,1)S(1)}, bf16[1,256,4096]{2,1,0:T(8,128)(2,1)S(1)}, bf16[1,64,4096]{2,1,0:T(8,128)(2,1)S(1)}, f32[1,4096]{1,0:T(1,128)S(1)}) custom-call(bf16[1,256,4096]{2,1,0:T(8,128)(2,1)} %arr.1, bf16[1,256,4096]{2,1,0:T(8,128)(2,1)} %grd.1, bf16[1,64,4096]{2,1,0:T(8,128)(2,1)} %sth.1, f32[1,4096]{1,0:T(1,128)} %gain.1, ...), custom_call_target="tpu_custom_call" | custom-call | flops 12348030976 | bytes 33554432 | tf_op jit(solution)/shard_map/pallas_call | solution.py:595
  79.1 2.3 %shard_map.121 = (bf16[1,256,4096]{2,1,0:T(8,128)(2,1)}, bf16[1,256,4096]{2,1,0:T(8,128)(2,1)}, bf16[1,64,4096]{2,1,0:T(8,128)(2,1)}, f32[1,4096]{1,0:T(1,128)}) custom-call(bf16[1,256,4096]{2,1,0:T(8,128)(2,1)S(1)} %get-tuple-element.8.f, bf16[1,256,4096]{2,1,0:T(8,128)(2,1)S(1)} %get-tuple-element.9.b, bf16[1,64,4096]{2,1,0:T(8,128)(2,1)S(1)} %get-tuple-element.10.e, ...), custom_call_target="tpu_custom_call" | custom-call | bytes 18874368 | tf_op jit(solution)/shard_map/pallas_call | solution.py:608

commit v4 on v3

--- a/solution.py
+++ b/solution.py
@@ -12,6 +12,7 @@
 LOG2E = 1.4426950408889634
 NC = 8
 EARLY = 3
+LAG = 3
 PAIR = 4
 NH = NC // 2
 EPSILON = 1e-05
@@ -395,9 +396,9 @@
     def run_out(n):
         sum_send(0, n, dot(ctx[...], wob[:, chunk(n)]))
 
-        @pl.when(n > 0)
+        @pl.when(n >= LAG)
         def _():
-            sum_core(n - 1)
+            sum_core(n - LAG)
 
         @pl.when(n == 2)
         def _():
@@ -406,7 +407,8 @@
         stash_forward(n)
 
     each(NC, run_out)
-    sum_core(NC - 1)
+    for n in range(NC - LAG, NC):
+        sum_core(n)
     each(NC, stash_last)
     normalize(zb)
     finish_f(0)
@@ -423,16 +425,19 @@
     def run_d_normed(n):
         sum_send(1, n, dot(dqkv[...], w[chunk(n), :], NT))
 
-        @pl.when(n > 0)
+        @pl.when(n >= LAG)
         def _():
-            sum_core_back(n - 1)
-
-            @pl.when(n % 2 == 0)
+            sum_core_back(n - LAG)
+
+            @pl.when((n - LAG) % 2 == 1)
             def _():
-                rs_lo(1, n // 2 - 1).start()
+                rs_lo(1, (n - LAG) // 2).start()
 
     each(NC, run_d_normed)
-    sum_core_back(NC - 1)
+    for n in range(NC - LAG, NC):
+        sum_core_back(n)
+        if n % 2 == 1 and n < NC - 1:
+            rs_lo(1, n // 2).start()
     for n in range(NH - 1, NC):
         rs_lo(1, n).start()
 

time: 81.5 us -> 81.5 us (level)
  no operation moved by 1% of the time
where the time goes in v4:
time: 81.5 us; the launch traced here: 81.4 us
  Pallas kernels  80.7 us (99%)
    pallas_call x1, Pallas kernels, shards(): pl.pallas_call(functools.partial(kernel, sections, tokens, width, heads),...  78.4 us
    pallas_call x1, Pallas kernels, shards(): pl.pallas_call(store, out_shape=tuple((pltpu.HBM(r.shape, r.dtype) for r...  2.3 us

profile of v4, /device:TPU:1, one launch (start us, length us, event | category | flops | bytes accessed | tf_op | source)
XLA Modules:
  0.0 81.4 jit_solution(16853348018559198300)
XLA Ops:
  0.6 78.4 %shard_map.120 = (bf16[1,256,4096]{2,1,0:T(8,128)(2,1)S(1)}, bf16[1,256,4096]{2,1,0:T(8,128)(2,1)S(1)}, bf16[1,64,4096]{2,1,0:T(8,128)(2,1)S(1)}, f32[1,4096]{1,0:T(1,128)S(1)}) custom-call(bf16[1,256,4096]{2,1,0:T(8,128)(2,1)} %arr.1, bf16[1,256,4096]{2,1,0:T(8,128)(2,1)} %grd.1, bf16[1,64,4096]{2,1,0:T(8,128)(2,1)} %sth.1, f32[1,4096]{1,0:T(1,128)} %gain.1, ...), custom_call_target="tpu_custom_call" | custom-call | flops 12348030976 | bytes 33554432 | tf_op jit(solution)/shard_map/pallas_call | solution.py:600
  79.1 2.3 %shard_map.121 = (bf16[1,256,4096]{2,1,0:T(8,128)(2,1)}, bf16[1,256,4096]{2,1,0:T(8,128)(2,1)}, bf16[1,64,4096]{2,1,0:T(8,128)(2,1)}, f32[1,4096]{1,0:T(1,128)}) custom-call(bf16[1,256,4096]{2,1,0:T(8,128)(2,1)S(1)} %get-tuple-element.8.f, bf16[1,256,4096]{2,1,0:T(8,128)(2,1)S(1)} %get-tuple-element.9.b, bf16[1,64,4096]{2,1,0:T(8,128)(2,1)S(1)} %get-tuple-element.10.e, ...), custom_call_target="tpu_custom_call" | custom-call | bytes 18874368 | tf_op jit(solution)/shard_map/pallas_call | solution.py:613
